TPU v7x, 32 devices: a whole 2x2x4 slice. The times are simulated.
32 devices in a mesh: dp: 4 (over y, x), mp: 8 (over z, core).
Axes of the slice: x: 2, y: 2, z: 4, core: 2. Of those that a mesh axis runs over, the one named last changes fastest.
Arguments:
- tokens: bfloat16 [8192, 2304], P(('dp', 'mp')), may hold values from -6 to 6
- ada_ffn: float32 [8, 2, 2304], P('dp'), may hold values from -4 to 4
- ffn_gate: float32 [8, 2304], P('dp'), may hold values from 0.5 to 1.5
- up_weight: bfloat16 [2304, 9216], P(None, 'mp'), may hold values from -0.125 to 0.125
- up_bias: float32 [9216], P('mp'), may hold values from -6 to 6
- down_weight: bfloat16 [9216, 2304], P('mp'), may hold values from -0.125 to 0.125
- down_bias: float32 [2304], replicated, may hold values from -6 to 6
- ada_head: float32 [8, 2, 2304], P('dp'), may hold values from -4 to 4
- head_weight: bfloat16 [2304, 4096], P(None, 'mp'), may hold values from -0.125 to 0.125
- head_bias: float32 [4096], P('mp'), may hold values from -6 to 6
- gumbel_noise: float32 [4, 1024, 4096], P('dp', None, 'mp'), as said below
- codebook: bfloat16 [4096, 32], P('mp'), may hold values from -16 to 16
- phi_weight: float32 [32, 32, 3, 3], replicated, may hold values from -0.375 to 0.375
- phi_bias: float32 [32], replicated, may hold values from -6 to 6
- f_hat: float32 [4, 32, 1024], P('dp', None, 'mp'), may hold values from -6 to 6
Outputs:
- block_out: bfloat16 [8192, 2304], P(('dp', 'mp'))
- f_hat_out: float32 [4, 32, 1024], P('dp', None, 'mp')
Inputs may be any that keep to these rules, and one draw needn't show every extreme that they name: `gumbel_noise`: noise added to the guided logits.
All inputs are finite; a program needn't handle non-finite values.
Results may differ from a plain program's by a relative error of at most 0.024.
Values may be sent and summed in bfloat16 or wider, within the bound.
No kernel may reach another device: no remote copies, remote signals or barrier semaphores. Data moves between devices by JAX's collectives and lax.ppermute only.
A program may use at most 256 MiB of HBM per device.

v0:
```python
import jax
import jax.numpy as jnp
from jax import lax
from jax.sharding import PartitionSpec as P

SIDE = 32
NEW = 1024


GUIDE = 1.5


def from_partner(value, axis, apart):
    mask = 2**apart
    pairs = [(source, source ^ mask) for source in range(lax.axis_size(axis))]
    return lax.ppermute(value, axis, pairs)


def norm_rows(values):
    row_mean = jnp.mean(values, axis=-1, keepdims=True)
    centred = values - row_mean
    spread = jnp.mean(centred * centred, axis=-1, keepdims=True)
    return centred * lax.rsqrt(spread + 1e-06)


def per_image(lookup, row_images):
    picked = jnp.broadcast_to(lookup[0], (row_images.shape[0],) + lookup.shape[1:])
    chosen = (row_images == 1).reshape((-1,) + (1,) * (lookup.ndim - 1))
    picked = jnp.where(chosen, lookup[1], picked)
    return picked


def modulate(values, ada_rows):
    return (norm_rows(values) * (1.0 + ada_rows[:, 1]) + ada_rows[:, 0]).astype(jnp.bfloat16)


def body(
    tokens,
    ada_ffn,
    ffn_gate,
    up_weight,
    up_bias,
    down_weight,
    down_bias,
    ada_head,
    head_weight,
    head_bias,
    gumbel_noise,
    codebook,
    phi_weight,
    phi_bias,
    f_hat,
):
    row_count = tokens.shape[0]
    shard_count = lax.axis_size("mp")
    mp_index = lax.axis_index("mp")
    group_rows = row_count * shard_count
    own_images = (mp_index * row_count + jnp.arange(row_count, dtype=jnp.int32)) // NEW
    gathered = lax.all_gather(tokens, "mp", axis=0, tiled=True)
    row_images = jnp.arange(group_rows, dtype=jnp.int32) // NEW
    full_hidden = jax.nn.gelu(
        jnp.dot(
            modulate(gathered.astype(jnp.float32), per_image(ada_ffn, row_images)),
            up_weight,
            preferred_element_type=jnp.float32,
        )
        + up_bias,
        approximate=True,
    ).astype(jnp.bfloat16)
    summed = lax.psum_scatter(
        jnp.dot(full_hidden, down_weight, preferred_element_type=jnp.float32),
        "mp",
        scatter_dimension=0,
        tiled=True,
    )
    block_out = (
        tokens.astype(jnp.float32) + per_image(ffn_gate, own_images) * (summed + down_bias)
    ).astype(jnp.bfloat16)
    full_out = lax.all_gather(block_out, "mp", axis=0, tiled=True)
    logits = (
        jnp.dot(
            modulate(full_out.astype(jnp.float32), per_image(ada_head, row_images)),
            head_weight,
            preferred_element_type=jnp.float32,
        )
        + head_bias
    )
    half_rows = group_rows // 2
    upper_half = lax.axis_index("dp") // (lax.axis_size("dp") // 2)
    kept_rows = lax.dynamic_slice_in_dim(logits, upper_half * half_rows, half_rows, 0)
    sent_rows = lax.dynamic_slice_in_dim(logits, (1 - upper_half) * half_rows, half_rows, 0)
    twin_rows = from_partner(sent_rows, "dp", lax.axis_size("dp").bit_length() - 2)
    cond_rows = jnp.where(upper_half == 0, kept_rows, twin_rows)
    uncond_rows = jnp.where(upper_half == 0, twin_rows, kept_rows)
    scores = (1.0 + GUIDE) * cond_rows - GUIDE * uncond_rows + gumbel_noise.reshape(half_rows, -1)
    row_peak = jnp.max(scores, axis=1)
    weights = jnp.exp(scores - row_peak[:, None]).astype(jnp.bfloat16)
    row_total = jnp.sum(weights.astype(jnp.float32), axis=1)
    mixed_code = jnp.dot(weights, codebook, preferred_element_type=jnp.float32)
    global_peak = lax.pmax(row_peak, "mp")
    factor = jnp.exp(row_peak - global_peak)
    row_total, mixed_code = (
        lax.psum((row_total * factor).astype(jnp.bfloat16), "mp").astype(jnp.float32),
        lax.psum((mixed_code * factor[:, None]).astype(jnp.bfloat16), "mp").astype(jnp.float32),
    )
    soft_code = mixed_code / row_total[:, None]
    pair_count = f_hat.shape[0]
    channels = f_hat.shape[1]
    band_rows = f_hat.shape[2] // SIDE
    code_maps = soft_code.reshape(pair_count, SIDE, SIDE, channels)
    padded = jnp.pad(code_maps, ((0, 0), (1, 1), (1, 1), (0, 0)))
    window = lax.dynamic_slice_in_dim(padded, mp_index * band_rows, band_rows + 2, 1)
    conv_out = (
        jnp.zeros((pair_count, channels, band_rows, SIDE), jnp.float32)
        + phi_bias[None, :, None, None]
    )
    for row_step in range(3):
        for col_step in range(3):
            conv_out = conv_out + jnp.einsum(
                "pyxc,oc->poyx",
                window[:, row_step : row_step + band_rows, col_step : col_step + SIDE, :],
                phi_weight[:, :, row_step, col_step],
                precision=lax.Precision.HIGHEST,
            )
    own_cells = jnp.transpose(window[:, 1 : band_rows + 1, 1 : SIDE + 1, :], (0, 3, 1, 2))
    f_hat_out = f_hat + (0.5 * own_cells + 0.5 * conv_out).reshape(
        pair_count, channels, band_rows * SIDE
    )
    return (block_out, f_hat_out)


def solution(mesh):
    in_specs = (
        P(("dp", "mp"), None),
        P("dp", None, None),
        P("dp", None),
        P(None, "mp"),
        P("mp"),
        P("mp", None),
        P(),
        P("dp", None, None),
        P(None, "mp"),
        P("mp"),
        P("dp", None, "mp"),
        P("mp", None),
        P(),
        P(),
        P("dp", None, "mp"),
    )
    out_specs = (P(("dp", "mp"), None), P("dp", None, "mp"))
    return jax.shard_map(body, mesh=mesh, in_specs=in_specs, out_specs=out_specs, check_vma=False)
```

profile of v0, /device:TPU:13, one launch (start us, length us, event | category | flops | bytes accessed | tf_op | source)
XLA Modules:
  0.0 585.8 jit_solution(17335645138088299447)
XLA Ops:
  7.2 0.0 copy-start
  7.2 0.0 all-gather.3.cloned.1.call-start
  7.2 0.7 all-gather.3.cloned.1.call-update
  7.9 0.0 reduce-scatter.2.cloned.1.call-start
  8.0 0.8 slice_bitcast_fusion.3
  8.8 25.9 %broadcast_select_fusion = (f32[2048,2,2304]{2,0,1:T(8,128)}, f32[2048,2,2304]{2,0,1:T(8,128)}) fusion(f32[2,2304]{1,0:T(2,128)S(1)} %get-tuple-element.9, f32[2,2304]{1,0:T(2,128)S(1)} %get-tuple-element.8, pred[2048]{0:T(1024)(128)(4,1)S(1)} %fusion.78, f32[2,2304]{1,0:T(2,128)S(1)} %get-tuple-element.14, f32[2,2304]{1,0:T(2,128)S(1)} %get-tuple-element.15), kind=kLoop, calls=%fused_computation.22 | loop fusion | flops 18874368 | bytes 75573248 | tf_op jit(solution)/shard_map/jit(_where)/select_n | solution.py:29
  34.6 64.8 %all-gather.3.cloned.1.call-done = bf16[2048,2304]{1,0:T(8,128)(2,1)} async-done(((bf16[256,2304]{1,0:T(8,128)(2,1)}), bf16[2048,2304]{1,0:T(8,128)(2,1)}) %all-gather.3.cloned.1.call-update) | async-done | bytes 9437200 | tf_op jit(solution)/shard_map/all_gather | solution.py:59
  99.4 5.1 convert_reduce_fusion.1
  104.6 1.2 copy-done.2
  105.8 2.6 fusion.8
  108.4 37.7 %fusion.27 = f32[2048,2304]{1,0:T(8,128)} fusion(bf16[1152,2304]{1,0:T(8,128)(2,1)} %param.20, bf16[2304,1152]{1,0:T(8,128)(2,1)} %param.18, bf16[2048,2304]{1,0:T(8,128)(2,1)} %all-gather.3.cloned.1.call-done, f32[2048,2,2304]{2,0,1:T(8,128)} %get-tuple-element.13, f32[2048]{0:T(1024)S(1)} %add_rsqrt_fusion.1, f32[2048]{0:T(1024)S(1)} %broadcast_multiply_fusion.1, ...), kind=kOutput, calls=%fused_computation.34 | convolution fusion | flops 21799895040 | bytes 76698112 | tf_op jit(solution)/shard_map/dot_general | solution.py:71
  146.1 0.0 reduce-scatter.2.cloned.1.call-update
  146.2 0.0 all-gather.5.cloned.1.call-start
  146.2 1.5 slice_reduce_fusion.1
  147.7 185.6 %reduce-scatter.2.cloned.1.call-done = f32[256,2304]{1,0:T(8,128)} async-done(((f32[2048,2304]{1,0:T(8,128)}), f32[256,2304]{1,0:T(8,128)}) %reduce-scatter.2.cloned.1.call-update) | async-done | bytes 2359312 | tf_op jit(solution)/shard_map/reduce_scatter | solution.py:70
  333.3 3.2 add_convert_fusion
  336.6 0.0 all-gather.5.cloned.1.call-update
  336.6 0.2 all-reduce.3.cloned.1.call-start
  336.9 88.4 %all-gather.5.cloned.1.call-done = bf16[2048,2304]{1,0:T(8,128)(2,1)} async-done(((bf16[256,2304]{1,0:T(8,128)(2,1)}), bf16[2048,2304]{1,0:T(8,128)(2,1)}) %all-gather.5.cloned.1.call-update) | async-done | bytes 9437200 | tf_op jit(solution)/shard_map/all_gather | solution.py:79
  425.2 5.1 convert_reduce_fusion
  430.4 1.2 copy-done.1
  431.6 2.6 fusion.4
  434.2 14.6 %fusion.36 = f32[2048,512]{0,1:T(8,128)S(1)} fusion(bf16[2304,512]{1,0:T(8,128)(2,1)S(1)} %copy-done, bf16[2048,2304]{1,0:T(8,128)(2,1)S(1)} %copy-done.1, f32[2048,2,2304]{2,0,1:T(8,128)} %get-tuple-element.12, f32[2048]{0:T(1024)S(1)} %add_rsqrt_fusion, f32[2048]{0:T(1024)S(1)} %broadcast_multiply_fusion, f32[512]{0:T(512)S(1)} %copy-done.10), kind=kOutput, calls=%fused_computation.41 | convolution fusion | flops 4865916928 | bytes 53757952 | tf_op jit(solution)/shard_map/dot_general | solution.py:81
  448.8 1.9 copy-done.4
  450.8 1.6 constant_dynamic-slice_fusion
  452.4 0.0 collective-permute-start
  452.4 3.0 copy.17
  455.4 44.2 %collective-permute-done = f32[1024,512]{0,1:T(8,128)} collective-permute-done((f32[1024,512]{0,1:T(8,128)}, f32[1024,512]{0,1:T(8,128)}, u32[]{:S(2)}, u32[]{:S(2)}) %collective-permute-start) | collective-permute-done | bytes 2097184 | tf_op jit(solution)/shard_map/ppermute | solution.py:16
  499.6 5.2 fusion.107
  504.9 13.0 %pmax.7 = f32[1024]{0:T(1024)S(1)} all-reduce(f32[1024]{0:T(1024)S(1)} %get-tuple-element.6), channel_id=1, replica_groups=mesh['dp'=4,'mp'=8] {'mp'}, use_global_device_ids=true, to_apply=%region_6.7 | all-reduce | flops 1024 | bytes 8192 | tf_op jit(solution)/shard_map/pmax | solution.py:100
  517.9 1.9 convert_reduce_fusion.2
  519.8 2.6 fusion.39
  522.5 0.0 all-reduce.3.cloned.1.call-update
  522.5 13.6 %psum.15 = bf16[1024]{0:T(1024)(128)(2,1)S(1)} all-reduce(bf16[1024]{0:T(1024)(128)(2,1)S(1)} %get-tuple-element.4), channel_id=1, replica_groups=mesh['dp'=4,'mp'=8] {'mp'}, use_global_device_ids=true, to_apply=%region_9.10 | all-reduce | flops 1024 | bytes 4096 | tf_op jit(solution)/shard_map/psum | solution.py:103
  536.1 39.5 %all-reduce.3.cloned.1.call-done = bf16[1024,32]{0,1:T(8,128)(2,1)} async-done(((bf16[1024,32]{0,1:T(8,128)(2,1)}), bf16[1024,32]{0,1:T(8,128)(2,1)}) %all-reduce.3.cloned.1.call-update) | async-done | bytes 65552 | tf_op jit(solution)/shard_map/psum | solution.py:104
  575.6 0.9 convert_divide_fusion
  576.5 0.2 copy.20
  576.7 0.2 convolution_add_fusion.8
  576.9 0.2 convolution_add_fusion.7
  577.1 0.2 convolution_add_fusion.6
  577.3 0.2 convolution_add_fusion.5
  577.6 0.2 convolution_add_fusion.4
  577.8 0.2 convolution_add_fusion.3
  578.0 0.2 convolution_add_fusion.2
  578.2 0.2 convolution_add_fusion.1
  578.4 0.2 fusion.42
  578.6 0.1 copy.19
  578.7 0.6 add.204
  (26 shorter events, 0.1 us)
Async XLA Ops:
  7.2 427.0 %copy-start = (bf16[2304,512]{1,0:T(8,128)(2,1)S(1)}, bf16[2304,512]{1,0:T(8,128)(2,1)}, u32[]{:S(2)}) copy-start(bf16[2304,512]{1,0:T(8,128)(2,1)} %param.23) | copy-start | bytes 7077892
  7.2 92.2 %all-gather.3.cloned.1.call-start = ((), (), s32[]{:S(2)}) async-start(), calls=%async_computation.1 | async-start | bytes 10616832 | tf_op jit(solution)/shard_map/all_gather | solution.py:59
  7.9 325.4 %reduce-scatter.2.cloned.1.call-start = ((), (), s32[]{:S(2)}) async-start(), calls=%async_computation.2 | async-start | bytes 21233664 | tf_op jit(solution)/shard_map/reduce_scatter | solution.py:70
  34.6 73.8 %copy-start.9 = (f32[1152]{0:T(1024)S(1)}, f32[1152]{0:T(1024)}, u32[]{:S(2)}) copy-start(f32[1152]{0:T(1024)} %param.19) | copy-start | bytes 13828
  99.4 6.4 %copy-start.2 = (bf16[2048,2304]{1,0:T(8,128)(2,1)S(1)}, bf16[2048,2304]{1,0:T(8,128)(2,1)}, u32[]{:S(2)}) copy-start(bf16[2048,2304]{1,0:T(8,128)(2,1)} %all-gather.3.cloned.1.call-done) | copy-start | bytes 28311556
  146.1 187.2 %copy-start.3 = (bf16[256,2304]{1,0:T(8,128)(2,1)S(1)}, bf16[256,2304]{1,0:T(8,128)(2,1)}, u32[]{:S(2)}) copy-start(bf16[256,2304]{1,0:T(8,128)(2,1)} %param.15) | copy-start | bytes 3538948
  146.2 279.1 %all-gather.5.cloned.1.call-start = ((), (), s32[]{:S(2)}) async-start(), calls=%async_computation.3 | async-start | bytes 10616832 | tf_op jit(solution)/shard_map/all_gather | solution.py:79
  336.6 239.0 %all-reduce.3.cloned.1.call-start = ((), (), s32[]{:S(2)}) async-start(), calls=%async_computation.4 | async-start | bytes 131072 | tf_op jit(solution)/shard_map/psum | solution.py:104
  336.8 97.4 %copy-start.10 = (f32[512]{0:T(512)S(1)}, f32[512]{0:T(512)}, u32[]{:S(2)}) copy-start(f32[512]{0:T(512)} %param.24) | copy-start | bytes 6148
  425.2 6.4 %copy-start.1 = (bf16[2048,2304]{1,0:T(8,128)(2,1)S(1)}, bf16[2048,2304]{1,0:T(8,128)(2,1)}, u32[]{:S(2)}) copy-start(bf16[2048,2304]{1,0:T(8,128)(2,1)} %all-gather.5.cloned.1.call-done) | copy-start | bytes 28311556
  448.8 1.9 copy-start.4
  450.8 69.1 %copy-start.6 = (bf16[512,32]{0,1:T(8,128)(2,1)S(1)}, bf16[512,32]{0,1:T(8,128)(2,1)}, u32[]{:S(2)}) copy-start(bf16[512,32]{0,1:T(8,128)(2,1)} %param.26) | copy-start | bytes 98308
  452.4 124.3 %copy-start.5 = (f32[32,32,3,3]{1,0,3,2:T(8,128)S(1)}, f32[32,32,3,3]{1,0,3,2:T(8,128)}, u32[]{:S(2)}) copy-start(f32[32,32,3,3]{1,0,3,2:T(8,128)} %param.27) | copy-start | bytes 110596
  452.4 124.3 %copy-start.8 = (f32[32]{0:T(128)S(1)}, f32[32]{0:T(128)}, u32[]{:S(2)}) copy-start(f32[32]{0:T(128)} %param.28) | copy-start | bytes 388
  452.4 47.3 %collective-permute-start = (f32[1024,512]{0,1:T(8,128)}, f32[1024,512]{0,1:T(8,128)}, u32[]{:S(2)}, u32[]{:S(2)}) collective-permute-start(f32[1024,512]{0,1:T(8,128)} %constant_dynamic-slice_fusion), channel_id=1, source_target_pairs={{0,16},{8,24},{16,0},{24,8},{1,17},{9,25},{17,1},{25,9},{2,18},{10... | collective-permute-start | bytes 6291464 | tf_op jit(solution)/shard_map/ppermute | solution.py:16
  455.4 123.3 %copy-start.7 = (f32[1,32,128]{2,1,0:T(8,128)S(1)}, f32[1,32,128]{2,1,0:T(8,128)}, u32[]{:S(2)}) copy-start(f32[1,32,128]{2,1,0:T(8,128)} %param.29) | copy-start | bytes 49156
Sparse Core Ops, SparseCore 0:
  9.7 89.7 all-gather.2
  146.3 187.0 reduce-scatter.1
  336.7 88.4 all-gather.4
  522.6 52.9 all-reduce.2
where the time goes:
time: 590 us; the launch traced here: 586 us
  waiting for transfers between devices  423 us (72%)
  matrix products  56.8 us (10%)
  other arithmetic  53.2 us (9%)
  blocking collectives  26.7 us (5%)
  between operations  14 us (2%)
  local copies, waits for them, and re-layouts  11.5 us (2%)
    reduce_scatter x1, waiting for transfers between devices, body(): lax.psum_scatter(jnp.dot(full_hidden, down_weight, preferred_element_type...  186 us
    all_gather x1, waiting for transfers between devices, body(): full_out = lax.all_gather(block_out, 'mp', axis=0, tiled=True)  88.4 us
    all_gather x1, waiting for transfers between devices, body(): gathered = lax.all_gather(tokens, 'mp', axis=0, tiled=True)  64.8 us
    ppermute x1, waiting for transfers between devices, from_partner(): return lax.ppermute(value, axis, pairs)  44.2 us
    psum x1, waiting for transfers between devices, body(): lax.psum((mixed_code * factor[:, None]).astype(jnp.bfloat16), 'mp')  39.5 us
    dot_general x1, matrix products, body(): jnp.dot(full_hidden, down_weight, preferred_element_type=jnp.float32)  37.7 us
    select_n x1, other arithmetic, per_image(): picked = jnp.where(chosen, lookup[1], picked)  25.9 us
    dot_general x1, matrix products, body(): jnp.dot(modulate(full_out.astype(jnp.float32), per_image(ada_head, row_im...  14.6 us
  transfers between devices with their start and end apart: 5, of which 5 were waited for; matrix products, arithmetic and copies ran while one was open for 5% of the time, Pallas kernels for 0%

commit v1 on v0

v1 whole, which is shorter than its diff:
```python
import jax
import jax.numpy as jnp
from jax import lax
from jax.sharding import PartitionSpec as P

SIDE = 32
NEW = 1024
GUIDE = 1.5
CHUNKS = 4
HEAD_CHUNKS = 2


def norm_rows(values):
    row_mean = jnp.mean(values, axis=-1, keepdims=True)
    centred = values - row_mean
    spread = jnp.mean(centred * centred, axis=-1, keepdims=True)
    return centred * lax.rsqrt(spread + 1e-06)


def modulate(values, ada):
    return norm_rows(values.astype(jnp.float32)) * (1.0 + ada[1]) + ada[0]


def permute_devices(value, dp, mp, target):
    pairs = []
    for d in range(dp):
        for m in range(mp):
            to = target(d, m)
            if to is not None:
                pairs.append((d * mp + m, to[0] * mp + to[1]))
    return lax.ppermute(value, ("dp", "mp"), pairs)


def body(
    tokens,
    ada_ffn,
    ffn_gate,
    up_weight,
    up_bias,
    down_weight,
    down_bias,
    ada_head,
    head_weight,
    head_bias,
    gumbel_noise,
    codebook,
    phi_weight,
    phi_bias,
    f_hat,
):
    rows, width = tokens.shape
    dp, mp = lax.axis_size("dp"), lax.axis_size("mp")
    d_index, m_index = lax.axis_index("dp"), lax.axis_index("mp")
    images = ada_ffn.shape[0]
    pairs = f_hat.shape[0]
    channels = f_hat.shape[1]
    vocab = head_weight.shape[1]
    own_image = (m_index * rows) // NEW
    ada_own = lax.dynamic_index_in_dim(ada_ffn, own_image, 0, keepdims=False)
    gate_own = lax.dynamic_index_in_dim(ffn_gate, own_image, 0, keepdims=False)
    head_own = lax.dynamic_index_in_dim(ada_head, own_image, 0, keepdims=False)
    half_dp, half_mp = dp // 2, mp // 2
    upper = d_index // half_dp

    def swap(d, m):
        return ((d + half_dp) % dp, m)

    def cross(d, m):
        if d // half_dp == m // half_mp:
            return None
        return ((d + half_dp) % dp, (m + half_mp) % mp)

    stays = upper == m_index // half_mp
    head_twin = permute_devices(head_own, dp, mp, swap)
    head_cond = jnp.where(upper == 0, head_own, head_twin)
    head_uncond = jnp.where(upper == 0, head_twin, head_own)

    step = rows // CHUNKS
    normed = modulate(tokens, ada_own).astype(jnp.bfloat16)
    outs = []
    for c in range(CHUNKS):
        part = lax.slice_in_dim(normed, c * step, (c + 1) * step, axis=0)
        gathered = lax.all_gather(part, "mp", axis=0, tiled=True)
        hidden = jax.nn.gelu(
            jnp.dot(gathered, up_weight, preferred_element_type=jnp.float32) + up_bias,
            approximate=True,
        ).astype(jnp.bfloat16)
        partial = jnp.dot(hidden, down_weight, preferred_element_type=jnp.float32).astype(jnp.bfloat16)
        summed = lax.psum_scatter(partial, "mp", scatter_dimension=0, tiled=True).astype(jnp.float32)
        own = lax.slice_in_dim(tokens, c * step, (c + 1) * step, axis=0).astype(jnp.float32)
        outs.append((own + gate_own * (summed + down_bias)).astype(jnp.bfloat16))
    block_out = jnp.concatenate(outs, axis=0)

    group = CHUNKS // HEAD_CHUNKS
    half = rows // HEAD_CHUNKS // 2
    noise = gumbel_noise.reshape(pairs, NEW // rows, HEAD_CHUNKS, 2, half, vocab)
    peaks, totals, codes = [], [], []
    for c in range(HEAD_CHUNKS):
        part = jnp.concatenate(outs[c * group : (c + 1) * group], axis=0)
        first, second = part[:half], part[half:]
        kept = jnp.where(upper == 0, first, second)
        sent = jnp.where(upper == 0, second, first)
        came = permute_devices(sent, dp, mp, swap)
        cond = jnp.where(upper == 0, kept, came)
        uncond = jnp.where(upper == 0, came, kept)
        mixed = (
            (1.0 + GUIDE) * modulate(cond, head_cond) - GUIDE * modulate(uncond, head_uncond)
        ).astype(jnp.bfloat16)
        crossed = permute_devices(mixed, dp, mp, cross)
        mixed = jnp.where(stays, mixed, crossed)
        gathered = lax.all_gather(mixed, "mp", axis=0, tiled=True)
        logits = jnp.dot(gathered, head_weight, preferred_element_type=jnp.float32) + head_bias
        logits = logits.reshape(2, half_mp, half, vocab)
        order = jnp.transpose(logits, (1, 0, 2, 3)).reshape(pairs, NEW // rows, 2, half, vocab)
        scores = order + noise[:, :, c]
        peak = jnp.max(scores, axis=-1)
        weights = jnp.exp(scores - peak[..., None]).astype(jnp.bfloat16)
        totals.append(jnp.sum(weights.astype(jnp.float32), axis=-1))
        codes.append(jnp.dot(weights, codebook, preferred_element_type=jnp.float32))
        peaks.append(peak)
    stack = lambda parts: jnp.stack(parts, axis=2)
    peak = stack(peaks).reshape(pairs, 1, NEW)
    total = stack(totals).reshape(pairs, 1, NEW)
    code = stack(codes).reshape(pairs, NEW, channels).transpose(0, 2, 1)
    stats = jnp.concatenate([code, total, peak], axis=1)

    cells = f_hat.shape[2]
    band = cells // SIDE
    padded = jnp.pad(stats, ((0, 0), (0, 0), (SIDE, SIDE)))
    windows = jnp.stack(
        [padded[:, :, m * cells : m * cells + cells + 2 * SIDE] for m in range(mp)], axis=0
    )
    parts = lax.all_to_all(windows, "mp", 0, 0, tiled=True)
    top = jnp.max(parts[:, :, channels + 1], axis=0)
    factor = jnp.exp(parts[:, :, channels + 1] - top[None])[:, :, None]
    sums = jnp.sum(parts[:, :, : channels + 1] * factor, axis=0)
    cell_index = m_index * cells - SIDE + jnp.arange(cells + 2 * SIDE)
    inside = (cell_index >= 0) & (cell_index < NEW)
    soft = jnp.where(inside, sums[:, :channels] / jnp.where(inside, sums[:, channels:], 1.0), 0.0)
    code_map = soft.reshape(pairs, channels, band + 2, SIDE)
    wide = jnp.pad(code_map, ((0, 0), (0, 0), (0, 0), (1, 1)))
    taps = jnp.stack(
        [wide[:, :, i : i + band, j : j + SIDE] for i in range(3) for j in range(3)], axis=2
    ).reshape(pairs, channels * 9, cells)
    conv = jnp.einsum(
        "ok,pkn->pon",
        phi_weight.reshape(channels, channels * 9),
        taps,
        precision=lax.Precision.HIGHEST,
        preferred_element_type=jnp.float32,
    ) + phi_bias[None, :, None]
    f_hat_out = f_hat + 0.5 * soft[:, :, SIDE : SIDE + cells] + 0.5 * conv
    return (block_out, f_hat_out)


def solution(mesh):
    in_specs = (
        P(("dp", "mp"), None),
        P("dp", None, None),
        P("dp", None),
        P(None, "mp"),
        P("mp"),
        P("mp", None),
        P(),
        P("dp", None, None),
        P(None, "mp"),
        P("mp"),
        P("dp", None, "mp"),
        P("mp", None),
        P(),
        P(),
        P("dp", None, "mp"),
    )
    out_specs = (P(("dp", "mp"), None), P("dp", None, "mp"))
    return jax.shard_map(body, mesh=mesh, in_specs=in_specs, out_specs=out_specs, check_vma=False)
```

time: 590 us -> 435 us (0.74)
  waiting for transfers between devices: 423 us -> 309 us
  other arithmetic: 53.2 us -> 17.7 us
  blocking collectives: 26.7 us -> 0 us
  starting transfers between devices: 0.38 us -> 21.1 us
    reduce_scatter x1 -> x4, waiting for transfers between devices: 186 us -> 131 us  [body(): lax.psum_scatter(partial, 'mp', scatter_dimension=0, tiled=True)]
    psum x1 -> x0, waiting for transfers between devices: 39.5 us -> none  [body(): lax.psum((mixed_code * factor[:, None]).astype(jnp.bfloat16), 'mp')]
    all_gather x2 -> x6, waiting for transfers between devices: 153 us -> 131 us  [the longest x4 90.2 us: body(): gathered = lax.all_gather(part, 'mp', axis=0, tiled=True)]
    select_n x1 -> x6, other arithmetic: 25.9 us -> 3.98 us  [the longest x1 1.74 us: body(): sent = jnp.where(upper == 0, second, first)]
    ppermute x1 -> x5, starting transfers between devices: 0.04 us -> 15.4 us  [permute_devices(): return lax.ppermute(value, ('dp', 'mp'), pairs)]
    psum x1 -> x0, blocking collectives: 13.6 us -> none  [body(): lax.psum((row_total * factor).astype(jnp.bfloat16), 'mp')]
    pmax x1 -> x0, blocking collectives: 13 us -> none  [body(): global_peak = lax.pmax(row_peak, 'mp')]
    reduce_sum x2 -> x3, other arithmetic: 10.2 us -> 2.26 us  [norm_rows(): row_mean = jnp.mean(values, axis=-1, keepdims=True)]
  transfers between devices with their start and end apart: 5 -> 16, of which waited for: 5 -> 15; matrix products, arithmetic and copies ran while one was open for 5% -> 14% of each run, Pallas kernels for 0% -> 0%
where the time goes in v1:
time: 435 us; the launch traced here: 431 us
  waiting for transfers between devices  309 us (71%)
  matrix products  58.4 us (13%)
  starting transfers between devices  21.1 us (5%)
  other arithmetic  17.7 us (4%)
  between operations  14.7 us (3%)
  local copies, waits for them, and re-layouts  10.5 us (2%)
    reduce_scatter x4, waiting for transfers between devices, body(): lax.psum_scatter(partial, 'mp', scatter_dimension=0, tiled=True)  131 us
    all_gather x4, waiting for transfers between devices, body(): gathered = lax.all_gather(part, 'mp', axis=0, tiled=True)  90.2 us
    dot_general x4, matrix products, body(): jnp.dot(hidden, down_weight, preferred_element_type=jnp.float32)  50.5 us
    all_gather x2, waiting for transfers between devices, body(): gathered = lax.all_gather(mixed, 'mp', axis=0, tiled=True)  40.8 us
    ppermute x5, waiting for transfers between devices, permute_devices(): return lax.ppermute(value, ('dp', 'mp'), pairs)  38.1 us
    ppermute x5, starting transfers between devices, permute_devices(): return lax.ppermute(value, ('dp', 'mp'), pairs)  15.4 us
  transfers between devices with their start and end apart: 16, of which 15 were waited for; matrix products, arithmetic and copies ran while one was open for 14% of the time, Pallas kernels for 0%

profile of v1, /device:TPU:13, one launch (start us, length us, event | category | flops | bytes accessed | tf_op | source)
XLA Modules:
  0.0 431.2 jit_solution(274716543026616388)
XLA Ops:
  7.3 1.7 convert_reduce_fusion
  9.0 1.7 fusion.2
  10.7 0.9 fusion.106
  12.1 1.0 fusion.125
  13.2 0.7 all-gather.7.cloned.1.call-update
  14.0 0.7 all-gather.9.cloned.1.call-update
  15.3 30.7 %all-gather.13.cloned.1.call-done = bf16[512,2304]{1,0:T(8,128)(2,1)} async-done(((bf16[64,2304]{1,0:T(8,128)(2,1)}), bf16[512,2304]{1,0:T(8,128)(2,1)}) %all-gather.13.cloned.1.call-update) | async-done | bytes 2359312 | tf_op jit(solution)/shard_map/all_gather | solution.py:83
  46.0 12.6 %convolution_convert_fusion = bf16[512,2304]{1,0:T(8,128)(2,1)} fusion(bf16[1152,2304]{1,0:T(8,128)(2,1)} %param.20, bf16[512,2304]{1,0:T(8,128)(2,1)} %all-gather.13.cloned.1.call-done, bf16[2304,1152]{1,0:T(8,128)(2,1)} %param.18, f32[1152]{0:T(1024)S(1)} %copy-done.18), kind=kOutput, calls=%fused_computation | convolution fusion | flops 5442895872 | bytes 15340032 | tf_op jit(solution)/shard_map/dot_general | solution.py:88
  58.7 19.7 %all-gather.7.cloned.1.call-done = bf16[512,2304]{1,0:T(8,128)(2,1)} async-done(((bf16[64,2304]{1,0:T(8,128)(2,1)}), bf16[512,2304]{1,0:T(8,128)(2,1)}) %all-gather.7.cloned.1.call-update) | async-done | bytes 2359312 | tf_op jit(solution)/shard_map/all_gather | solution.py:83
  78.4 12.6 %convolution_convert_fusion.3 = bf16[512,2304]{1,0:T(8,128)(2,1)} fusion(bf16[1152,2304]{1,0:T(8,128)(2,1)} %param.20, bf16[512,2304]{1,0:T(8,128)(2,1)} %all-gather.7.cloned.1.call-done, bf16[2304,1152]{1,0:T(8,128)(2,1)} %param.18, f32[1152]{0:T(1024)S(1)} %copy-done.18), kind=kOutput, calls=%fused_computation.3 | convolution fusion | flops 5442895872 | bytes 15340032 | tf_op jit(solution)/shard_map/dot_general | solution.py:88
  91.3 20.1 %all-gather.9.cloned.1.call-done = bf16[512,2304]{1,0:T(8,128)(2,1)} async-done(((bf16[64,2304]{1,0:T(8,128)(2,1)}), bf16[512,2304]{1,0:T(8,128)(2,1)}) %all-gather.9.cloned.1.call-update) | async-done | bytes 2359312 | tf_op jit(solution)/shard_map/all_gather | solution.py:83
  111.4 12.6 %convolution_convert_fusion.2 = bf16[512,2304]{1,0:T(8,128)(2,1)} fusion(bf16[1152,2304]{1,0:T(8,128)(2,1)} %param.20, bf16[512,2304]{1,0:T(8,128)(2,1)} %all-gather.9.cloned.1.call-done, bf16[2304,1152]{1,0:T(8,128)(2,1)} %param.18, f32[1152]{0:T(1024)S(1)} %copy-done.18), kind=kOutput, calls=%fused_computation.2 | convolution fusion | flops 5442895872 | bytes 15340032 | tf_op jit(solution)/shard_map/dot_general | solution.py:88
  124.1 19.6 %all-gather.11.cloned.1.call-done = bf16[512,2304]{1,0:T(8,128)(2,1)} async-done(((bf16[64,2304]{1,0:T(8,128)(2,1)}), bf16[512,2304]{1,0:T(8,128)(2,1)}) %all-gather.11.cloned.1.call-update) | async-done | bytes 2359312 | tf_op jit(solution)/shard_map/all_gather | solution.py:83
  143.7 12.6 %convolution_convert_fusion.1 = bf16[512,2304]{1,0:T(8,128)(2,1)} fusion(bf16[1152,2304]{1,0:T(8,128)(2,1)} %param.20, bf16[512,2304]{1,0:T(8,128)(2,1)} %all-gather.11.cloned.1.call-done, bf16[2304,1152]{1,0:T(8,128)(2,1)} %param.18, f32[1152]{0:T(1024)S(1)} %copy-done.18), kind=kOutput, calls=%fused_computation.1 | convolution fusion | flops 5442895872 | bytes 15340032 | tf_op jit(solution)/shard_map/dot_general | solution.py:88
  156.6 1.3 dynamic-slice_bitcast_fusion
  158.2 0.8 dynamic-slice_reduce_fusion.1
  159.0 17.9 %reduce-scatter.11.cloned.1.call-done = bf16[64,2304]{1,0:T(8,128)(2,1)} async-done(((bf16[512,2304]{1,0:T(8,128)(2,1)}), bf16[64,2304]{1,0:T(8,128)(2,1)}) %reduce-scatter.11.cloned.1.call-update) | async-done | bytes 294928 | tf_op jit(solution)/shard_map/reduce_scatter | solution.py:89
  176.9 37.7 %reduce-scatter.5.cloned.1.call-done = bf16[64,2304]{1,0:T(8,128)(2,1)} async-done(((bf16[512,2304]{1,0:T(8,128)(2,1)}), bf16[64,2304]{1,0:T(8,128)(2,1)}) %reduce-scatter.5.cloned.1.call-update) | async-done | bytes 294928 | tf_op jit(solution)/shard_map/reduce_scatter | solution.py:89
  214.6 38.1 %reduce-scatter.7.cloned.1.call-done = bf16[64,2304]{1,0:T(8,128)(2,1)} async-done(((bf16[512,2304]{1,0:T(8,128)(2,1)}), bf16[64,2304]{1,0:T(8,128)(2,1)}) %reduce-scatter.7.cloned.1.call-update) | async-done | bytes 294928 | tf_op jit(solution)/shard_map/reduce_scatter | solution.py:89
  252.7 37.8 %reduce-scatter.9.cloned.1.call-done = bf16[64,2304]{1,0:T(8,128)(2,1)} async-done(((bf16[512,2304]{1,0:T(8,128)(2,1)}), bf16[64,2304]{1,0:T(8,128)(2,1)}) %reduce-scatter.9.cloned.1.call-update) | async-done | bytes 294928 | tf_op jit(solution)/shard_map/reduce_scatter | solution.py:89
  290.4 1.7 broadcast_select_fusion.6
  292.7 0.7 broadcast_select_fusion.11
  293.5 1.1 collective-permute-start.3
  294.6 4.4 %collective-permute-done = bf16[64,2304]{1,0:T(8,128)(2,1)S(1)} collective-permute-done((bf16[64,2304]{1,0:T(8,128)(2,1)S(1)}, bf16[64,2304]{1,0:T(8,128)(2,1)S(1)}, u32[]{:S(2)}, u32[]{:S(2)}) %collective-permute-start) | collective-permute-done | bytes 294944 | tf_op jit(solution)/shard_map/ppermute | solution.py:31
  299.7 5.7 %collective-permute-done.3 = bf16[64,2304]{1,0:T(8,128)(2,1)S(1)} collective-permute-done((bf16[64,2304]{1,0:T(8,128)(2,1)S(1)}, bf16[64,2304]{1,0:T(8,128)(2,1)S(1)}, u32[]{:S(2)}, u32[]{:S(2)}) %collective-permute-start.3) | collective-permute-done | bytes 294944 | tf_op jit(solution)/shard_map/ppermute | solution.py:31
  306.7 7.7 %collective-permute-start.4 = (bf16[64,2304]{1,0:T(8,128)(2,1)S(1)}, bf16[64,2304]{1,0:T(8,128)(2,1)S(1)}, u32[]{:S(2)}, u32[]{:S(2)}) collective-permute-start(bf16[64,2304]{1,0:T(8,128)(2,1)S(1)} %get-tuple-element.43), channel_id=1, source_target_pairs={{4,16},{5,17},{6,18},{7,19},{12,24},{13,25},{14,26},{15,27},{16,4}... | collective-permute-start | bytes 884744 | tf_op jit(solution)/shard_map/ppermute | solution.py:31
  314.5 10.9 %collective-permute-done.4 = bf16[64,2304]{1,0:T(8,128)(2,1)S(1)} collective-permute-done((bf16[64,2304]{1,0:T(8,128)(2,1)S(1)}, bf16[64,2304]{1,0:T(8,128)(2,1)S(1)}, u32[]{:S(2)}, u32[]{:S(2)}) %collective-permute-start.4) | collective-permute-done | bytes 294944 | tf_op jit(solution)/shard_map/ppermute | solution.py:31
  325.4 0.7 broadcast_select_fusion.8
  326.2 5.8 %collective-permute-start.2 = (bf16[64,2304]{1,0:T(8,128)(2,1)S(1)}, bf16[64,2304]{1,0:T(8,128)(2,1)S(1)}, u32[]{:S(2)}, u32[]{:S(2)}) collective-permute-start(bf16[64,2304]{1,0:T(8,128)(2,1)S(1)} %get-tuple-element.44), channel_id=1, source_target_pairs={{4,16},{5,17},{6,18},{7,19},{12,24},{13,25},{14,26},{15,27},{16,4}... | collective-permute-start | bytes 884744 | tf_op jit(solution)/shard_map/ppermute | solution.py:31
  332.0 17.1 %collective-permute-done.2 = bf16[64,2304]{1,0:T(8,128)(2,1)S(1)} collective-permute-done((bf16[64,2304]{1,0:T(8,128)(2,1)S(1)}, bf16[64,2304]{1,0:T(8,128)(2,1)S(1)}, u32[]{:S(2)}, u32[]{:S(2)}) %collective-permute-start.2) | collective-permute-done | bytes 294944 | tf_op jit(solution)/shard_map/ppermute | solution.py:31
  349.1 0.7 broadcast_select_fusion.9
  350.1 0.7 reshape.190
  351.3 12.3 %all-gather.17.cloned.1.call-done = bf16[512,2304]{1,0:T(8,128)(2,1)} async-done(((bf16[64,2304]{1,0:T(8,128)(2,1)}), bf16[512,2304]{1,0:T(8,128)(2,1)}) %all-gather.17.cloned.1.call-update) | async-done | bytes 2359312 | tf_op jit(solution)/shard_map/all_gather | solution.py:111
  363.7 3.0 convolution_add_fusion.4
  366.7 28.5 %all-gather.15.cloned.1.call-done = bf16[512,2304]{1,0:T(8,128)(2,1)} async-done(((bf16[64,2304]{1,0:T(8,128)(2,1)}), bf16[512,2304]{1,0:T(8,128)(2,1)}) %all-gather.15.cloned.1.call-update) | async-done | bytes 2359312 | tf_op jit(solution)/shard_map/all_gather | solution.py:111
  395.2 3.2 convolution_add_fusion.5
  398.8 1.2 convert_reduce_fusion.2
  400.8 0.9 copy.32
  401.7 1.9 reshape.185
  403.6 0.7 pad_maximum_fusion.3
  405.0 0.9 pad_maximum_fusion.2
  406.6 1.0 copy.33
  407.6 4.8 %all-to-all-start = ((f32[8,1,34,192]{3,1,2,0:T(1,128)}), f32[8,1,34,192]{3,1,2,0:T(1,128)}, u32[]{:S(2)}, u32[]{:S(2)}) async-start(f32[8,1,34,192]{3,1,2,0:T(1,128)} %copy.33), calls=%async_computation.4 | async-start | bytes 557056 | tf_op jit(solution)/shard_map/all_to_all | solution.py:133
  412.5 1.1 pad_maximum_fusion
  413.6 6.5 %all-to-all-done = f32[8,1,34,192]{3,1,2,0:T(1,128)} async-done(((f32[8,1,34,192]{3,1,2,0:T(1,128)}), f32[8,1,34,192]{3,1,2,0:T(1,128)}, u32[]{:S(2)}, u32[]{:S(2)}) %all-to-all-start) | async-done | bytes 208928 | tf_op jit(solution)/shard_map/all_to_all | solution.py:133
  420.0 0.7 slice_reduce_fusion.2
  420.8 1.3 fusion.74
  423.4 1.0 fusion.41
  (110 shorter events, 9.2 us)
Async XLA Ops:
  7.2 356.5 %copy-start = (bf16[2304,512]{1,0:T(8,128)(2,1)S(1)}, bf16[2304,512]{1,0:T(8,128)(2,1)}, u32[]{:S(2)}) copy-start(bf16[2304,512]{1,0:T(8,128)(2,1)} %param.23) | copy-start | bytes 7077892
  7.2 4.4 %copy-start.1 = (bf16[256,2304]{1,0:T(8,128)(2,1)S(1)}, bf16[256,2304]{1,0:T(8,128)(2,1)}, u32[]{:S(2)}) copy-start(bf16[256,2304]{1,0:T(8,128)(2,1)} %param.15) | copy-start | bytes 3538948
  7.2 38.8 %all-gather.13.cloned.1.call-start = ((), (), s32[]{:S(2)}) async-start(), calls=%async_computation.11 | async-start | bytes 2654208 | tf_op jit(solution)/shard_map/all_gather | solution.py:83
  12.1 33.9 %copy-start.18 = (f32[1152]{0:T(1024)S(1)}, f32[1152]{0:T(1024)}, u32[]{:S(2)}) copy-start(f32[1152]{0:T(1024)} %param.19) | copy-start | bytes 13828
  13.2 65.2 %all-gather.7.cloned.1.call-start = ((), (), s32[]{:S(2)}) async-start(), calls=%async_computation.5 | async-start | bytes 2654208 | tf_op jit(solution)/shard_map/all_gather | solution.py:83
  13.9 97.5 %all-gather.9.cloned.1.call-start = ((), (), s32[]{:S(2)}) async-start(), calls=%async_computation.7 | async-start | bytes 2654208 | tf_op jit(solution)/shard_map/all_gather | solution.py:83
  14.7 129.0 %all-gather.11.cloned.1.call-start = ((), (), s32[]{:S(2)}) async-start(), calls=%async_computation.9 | async-start | bytes 2654208 | tf_op jit(solution)/shard_map/all_gather | solution.py:83
  15.2 161.7 %reduce-scatter.11.cloned.1.call-start = ((), (), s32[]{:S(2)}) async-start(), calls=%async_computation.12 | async-start | bytes 2654208 | tf_op jit(solution)/shard_map/reduce_scatter | solution.py:89
  58.6 156.0 %reduce-scatter.5.cloned.1.call-start = ((), (), s32[]{:S(2)}) async-start(), calls=%async_computation.6 | async-start | bytes 2654208 | tf_op jit(solution)/shard_map/reduce_scatter | solution.py:89
  91.1 161.6 %reduce-scatter.7.cloned.1.call-start = ((), (), s32[]{:S(2)}) async-start(), calls=%async_computation.8 | async-start | bytes 2654208 | tf_op jit(solution)/shard_map/reduce_scatter | solution.py:89
  124.0 166.4 %reduce-scatter.9.cloned.1.call-start = ((), (), s32[]{:S(2)}) async-start(), calls=%async_computation.10 | async-start | bytes 2654208 | tf_op jit(solution)/shard_map/reduce_scatter | solution.py:89
  156.3 207.3 %all-gather.17.cloned.1.call-start = ((), (), s32[]{:S(2)}) async-start(), calls=%async_computation.14 | async-start | bytes 2654208 | tf_op jit(solution)/shard_map/all_gather | solution.py:111
  157.9 134.7 %collective-permute-start.1 = (f32[2,2304]{1,0:T(2,128)}, f32[2,2304]{1,0:T(2,128)}, u32[]{:S(2)}, u32[]{:S(2)}) collective-permute-start(f32[2,2304]{1,0:T(2,128)} %dynamic-slice_bitcast_fusion), channel_id=1, source_target_pairs={{0,16},{1,17},{2,18},{3,19},{4,20},{5,21},{6,22},{7,23},{8,24},{9,... | collective-permute-start | bytes 55304 | tf_op jit(solution)/shard_map/ppermute | solution.py:31
  290.4 2.3 copy-start.14
  292.2 14.5 %copy-start.3 = (bf16[64,2304]{1,0:T(8,128)(2,1)}, bf16[64,2304]{1,0:T(8,128)(2,1)S(1)}, u32[]{:S(2)}) copy-start(bf16[64,2304]{1,0:T(8,128)(2,1)S(1)} %get-tuple-element.26) | copy-start | bytes 884740
  292.2 14.5 %copy-start.5 = (bf16[64,2304]{1,0:T(8,128)(2,1)}, bf16[64,2304]{1,0:T(8,128)(2,1)S(1)}, u32[]{:S(2)}) copy-start(bf16[64,2304]{1,0:T(8,128)(2,1)S(1)} %get-tuple-element.27) | copy-start | bytes 884740
  292.2 14.5 %copy-start.7 = (bf16[64,2304]{1,0:T(8,128)(2,1)}, bf16[64,2304]{1,0:T(8,128)(2,1)S(1)}, u32[]{:S(2)}) copy-start(bf16[64,2304]{1,0:T(8,128)(2,1)S(1)} %get-tuple-element.31) | copy-start | bytes 884740
  292.2 14.5 %copy-start.9 = (bf16[64,2304]{1,0:T(8,128)(2,1)}, bf16[64,2304]{1,0:T(8,128)(2,1)S(1)}, u32[]{:S(2)}) copy-start(bf16[64,2304]{1,0:T(8,128)(2,1)S(1)} %get-tuple-element.32) | copy-start | bytes 884740
  292.2 6.8 %collective-permute-start = (bf16[64,2304]{1,0:T(8,128)(2,1)S(1)}, bf16[64,2304]{1,0:T(8,128)(2,1)S(1)}, u32[]{:S(2)}, u32[]{:S(2)}) collective-permute-start(bf16[64,2304]{1,0:T(8,128)(2,1)S(1)} %get-tuple-element.25), channel_id=1, source_target_pairs={{0,16},{1,17},{2,18},{3,19},{4,20},{5,21},{6,22},{7,23},{8,24},{9,... | collective-permute-start | bytes 884744 | tf_op jit(solution)/shard_map/ppermute | solution.py:31
  293.5 11.8 %collective-permute-start.3 = (bf16[64,2304]{1,0:T(8,128)(2,1)S(1)}, bf16[64,2304]{1,0:T(8,128)(2,1)S(1)}, u32[]{:S(2)}, u32[]{:S(2)}) collective-permute-start(bf16[64,2304]{1,0:T(8,128)(2,1)S(1)} %get-tuple-element.30), channel_id=1, source_target_pairs={{0,16},{1,17},{2,18},{3,19},{4,20},{5,21},{6,22},{7,23},{8,24},{9,... | collective-permute-start | bytes 884744 | tf_op jit(solution)/shard_map/ppermute | solution.py:31
  305.6 44.3 %copy-start.12 = (f32[32,32,3,3]{1,0,3,2:T(8,128)S(1)}, f32[32,32,3,3]{1,0,3,2:T(8,128)}, u32[]{:S(2)}) copy-start(f32[32,32,3,3]{1,0,3,2:T(8,128)} %param.27) | copy-start | bytes 110596
  306.0 57.7 %copy-start.19 = (f32[512]{0:T(512)S(1)}, f32[512]{0:T(512)}, u32[]{:S(2)}) copy-start(f32[512]{0:T(512)} %param.24) | copy-start | bytes 6148
  306.7 18.7 %collective-permute-start.4 = (bf16[64,2304]{1,0:T(8,128)(2,1)S(1)}, bf16[64,2304]{1,0:T(8,128)(2,1)S(1)}, u32[]{:S(2)}, u32[]{:S(2)}) collective-permute-start(bf16[64,2304]{1,0:T(8,128)(2,1)S(1)} %get-tuple-element.43), channel_id=1, source_target_pairs={{4,16},{5,17},{6,18},{7,19},{12,24},{13,25},{14,26},{15,27},{16,4}... | collective-permute-start | bytes 884744 | tf_op jit(solution)/shard_map/ppermute | solution.py:31
  326.2 69.1 %all-gather.15.cloned.1.call-start = ((), (), s32[]{:S(2)}) async-start(), calls=%async_computation.13 | async-start | bytes 2654208 | tf_op jit(solution)/shard_map/all_gather | solution.py:111
  326.2 22.9 %collective-permute-start.2 = (bf16[64,2304]{1,0:T(8,128)(2,1)S(1)}, bf16[64,2304]{1,0:T(8,128)(2,1)S(1)}, u32[]{:S(2)}, u32[]{:S(2)}) collective-permute-start(bf16[64,2304]{1,0:T(8,128)(2,1)S(1)} %get-tuple-element.44), channel_id=1, source_target_pairs={{4,16},{5,17},{6,18},{7,19},{12,24},{13,25},{14,26},{15,27},{16,4}... | collective-permute-start | bytes 884744 | tf_op jit(solution)/shard_map/ppermute | solution.py:31
  395.2 3.2 copy-start.2
  398.8 1.2 copy-start.13
  400.4 12.1 %copy-start.4 = (bf16[64,2304]{1,0:T(8,128)(2,1)S(1)}, bf16[64,2304]{1,0:T(8,128)(2,1)}, u32[]{:S(2)}) copy-start(bf16[64,2304]{1,0:T(8,128)(2,1)} %copy-done.3) | copy-start | bytes 884740
  400.4 12.1 %copy-start.6 = (bf16[64,2304]{1,0:T(8,128)(2,1)S(1)}, bf16[64,2304]{1,0:T(8,128)(2,1)}, u32[]{:S(2)}) copy-start(bf16[64,2304]{1,0:T(8,128)(2,1)} %copy-done.5) | copy-start | bytes 884740
  400.4 12.1 %copy-start.8 = (bf16[64,2304]{1,0:T(8,128)(2,1)S(1)}, bf16[64,2304]{1,0:T(8,128)(2,1)}, u32[]{:S(2)}) copy-start(bf16[64,2304]{1,0:T(8,128)(2,1)} %copy-done.7) | copy-start | bytes 884740
  400.4 12.1 %copy-start.10 = (bf16[64,2304]{1,0:T(8,128)(2,1)S(1)}, bf16[64,2304]{1,0:T(8,128)(2,1)}, u32[]{:S(2)}) copy-start(bf16[64,2304]{1,0:T(8,128)(2,1)} %copy-done.9) | copy-start | bytes 884740
  406.0 16.1 %copy-start.17 = (pred[192]{0:T(512)(128)(4,1)S(1)}, pred[192]{0:T(512)(128)(4,1)}, u32[]{:S(2)}) copy-start(pred[192]{0:T(512)(128)(4,1)} %compare_and_fusion) | copy-start | bytes 580
  407.6 12.4 %all-to-all-start = ((f32[8,1,34,192]{3,1,2,0:T(1,128)}), f32[8,1,34,192]{3,1,2,0:T(1,128)}, u32[]{:S(2)}, u32[]{:S(2)}) async-start(f32[8,1,34,192]{3,1,2,0:T(1,128)} %copy.33), calls=%async_computation.4 | async-start | bytes 557056 | tf_op jit(solution)/shard_map/all_to_all | solution.py:133
  413.6 9.8 %copy-start.11 = (f32[32,288]{0,1:T(8,128)S(1)}, f32[32,288]{0,1:T(8,128)}, u32[]{:S(2)}) copy-start(f32[32,288]{0,1:T(8,128)} %reshape.190) | copy-start | bytes 110596
  413.6 9.8 %copy-start.15 = (f32[1,32,128]{2,1,0:T(8,128)S(1)}, f32[1,32,128]{2,1,0:T(8,128)}, u32[]{:S(2)}) copy-start(f32[1,32,128]{2,1,0:T(8,128)} %param.29) | copy-start | bytes 49156
  413.6 9.8 %copy-start.16 = (f32[32]{0:T(128)S(1)}, f32[32]{0:T(128)}, u32[]{:S(2)}) copy-start(f32[32]{0:T(128)} %param.28) | copy-start | bytes 388
Sparse Core Ops, SparseCore 0:
  13.3 32.6 all-gather.12
  47.6 30.7 all-gather.6
  80.6 30.7 all-gather.8
  112.9 30.7 all-gather.10
  145.8 31.0 reduce-scatter.10
  179.1 35.4 reduce-scatter.4
  216.9 35.7 reduce-scatter.6
  255.0 35.3 reduce-scatter.8
  326.3 37.3 all-gather.16
  365.2 30.0 all-gather.14
